TPU v7x, 256 devices: a whole 4x4x8 slice. The times are simulated.
256 devices in a mesh: leaf: 32 (over z, y), panel: 8 (over x, core).
Axes of the slice: x: 4, y: 4, z: 8, core: 2. Of those that a mesh axis runs over, the one named last changes fastest.
Arguments:
- interface_block: float32 [32, 2048, 2048], P('leaf', 'panel'), may hold values from -0.125 to 0.125
- coupling: bfloat16 [32, 2048, 128], P('leaf', 'panel'), may hold values from -0.375 to 0.375
- eigenvalues: float32 [32, 128], P('leaf'), may hold values from 0.5 to 8
- mode_counts: int32 [32], P('leaf'), may hold values from 64 to 128, as said below
- interface_coords: bfloat16 [32, 2048, 1024], P('leaf', 'panel'), may hold values from -6 to 6
- modal_coords: bfloat16 [32, 128, 4096], P('leaf'), may hold values from -6 to 6
Outputs:
- mode_shapes: float32 [32, 2048, 1024], P('leaf', 'panel')
Inputs may be any that keep to these rules, and one draw needn't show every extreme that they name: `mode_counts`: modes kept by each substructure; some substructure keeps all 128.
All inputs are finite; a program needn't handle non-finite values.
Results may differ from a plain program's by a relative error of at most 0.0023.
Values may be sent and summed in bfloat16 or wider, within the bound.
A program may use at most 128 MiB of HBM per device.

v0:
```python
import jax
import jax.numpy as jnp
from jax import lax
from jax.sharding import PartitionSpec as P

LEVELS = 2


def partner(value, axis, bit):
    return lax.ppermute(value, axis, [(i, i ^ 1 << bit) for i in range(lax.axis_size(axis))])


def modal_reduce(summed, levels):
    leaf_index = lax.axis_index("leaf")
    current = summed
    for level in range(levels - 1, -1, -1):
        half = current.shape[1] // 2
        my_bit = leaf_index >> level & 1
        keep = lax.dynamic_slice_in_dim(current, my_bit * half, half, 1)
        other = lax.dynamic_slice_in_dim(current, (1 - my_bit) * half, half, 1)
        current = keep + partner(other, "leaf", level)
    return current


def on_device(interface_block, coupling, eigenvalues, mode_counts, interface_coords, modal_coords):
    block = interface_block[0]
    coup = coupling[0]
    coords = interface_coords[0]
    modal = modal_coords[0]
    width = coup.shape[1]
    levels = LEVELS
    index = jnp.arange(width, dtype=jnp.int32)
    mask = (index < mode_counts[0]).astype(jnp.float32)
    scaled = (coup.astype(jnp.float32) * (mask / eigenvalues[0])[None, :]).astype(jnp.bfloat16)
    columns = block
    schur = columns - lax.dot_general(
        scaled,
        lax.all_gather(coup, "panel", axis=0, tiled=True),
        (((1,), (1,)), ((), ())),
        preferred_element_type=jnp.float32,
    )
    merged = schur
    for level in range(levels):
        merged = merged + partner(merged, "leaf", level)
    owned = modal_reduce(jnp.dot(scaled, modal, preferred_element_type=jnp.float32), levels)
    columns = merged
    shapes = owned + jnp.dot(
        columns,
        lax.all_gather(coords, "panel", axis=0, tiled=True).astype(jnp.float32),
        precision=lax.Precision.HIGHEST,
    )
    return shapes[None]


def solution(mesh):
    placed = (
        P("leaf", "panel", None),
        P("leaf", "panel", None),
        P("leaf", None),
        P("leaf"),
        P("leaf", "panel", None),
        P("leaf", None, None),
    )
    return jax.shard_map(
        on_device, mesh=mesh, in_specs=placed, out_specs=P("leaf", "panel", None), check_vma=False
    )
```

profile of v0, /device:TPU:1, one launch (start us, length us, event | category | flops | bytes accessed | tf_op | source)
XLA Modules:
  0.0 201.7 jit_solution(3715530566430641036)
XLA Ops:
  6.5 0.0 copy-start
  6.5 0.0 all-gather.4.cloned.1.call-start
  6.5 0.7 all-gather.4.cloned.1.call-update
  7.9 0.7 fusion.15
  8.6 16.4 %all-gather = bf16[1,2048,128]{2,1,0:T(8,128)(2,1)S(1)} all-gather(bf16[1,256,128]{2,1,0:T(8,128)(2,1)} %param.7), channel_id=2, replica_groups=mesh['leaf'=32,'panel'=8] {'panel'}, dimensions={1}, use_global_device_ids=true | all-gather | bytes 589824 | tf_op jit(solution)/shard_map/all_gather | solution.py:38
  25.0 0.0 copy-start.1
  25.0 2.2 %convolution_subtract_fusion = f32[256,2048]{1,0:T(8,128)S(1)} fusion(f32[1,256,2048]{2,1,0:T(8,128)} %param.6, bf16[1,2048,128]{2,1,0:T(8,128)(2,1)S(1)} %all-gather, bf16[1,256,128]{2,1,0:T(8,128)(2,1)} %param.7, f32[128]{0:T(128)S(1)} %fusion.15), kind=kOutput, calls=%fused_computation.2 | convolution fusion | flops 134840320 | bytes 4784640 | tf_op jit(solution)/shard_map/dot_general | solution.py:36
  27.2 0.1 collective-permute-start.2
  27.3 0.0 copy-done
  27.3 0.0 copy-done.1
  27.3 2.7 %fusion.3 = f32[256,4096]{1,0:T(8,128)} fusion(bf16[1,128,4096]{2,1,0:T(8,128)(2,1)S(1)} %copy-done, bf16[1,256,128]{2,1,0:T(8,128)(2,1)S(1)} %copy-done.1, f32[128]{0:T(128)S(1)} %fusion.15), kind=kOutput, calls=%fused_computation.5 | convolution fusion | flops 268533760 | bytes 5308928 | tf_op jit(solution)/shard_map/dot_general | solution.py:45
  30.0 3.1 %constant_dynamic-slice_fusion.1 = f32[256,2048]{1,0:T(8,128)} fusion(f32[256,4096]{1,0:T(8,128)} %fusion.3, s32[]{:T(128)S(6)} %select_n.13), kind=kLoop, calls=%fused_computation.19 | loop fusion | bytes 4194308 | tf_op jit(solution)/shard_map/dynamic_slice | solution.py:20
  33.1 2.5 %collective-permute-start = (f32[256,2048]{1,0:T(8,128)}, f32[256,2048]{1,0:T(8,128)}, u32[]{:S(2)}, u32[]{:S(2)}) collective-permute-start(f32[256,2048]{1,0:T(8,128)} %constant_dynamic-slice_fusion.1), channel_id=1, source_target_pairs={{0,16},{8,24},{16,0},{24,8},{32,48},{40,56},{48,32},{56,40},{64,80... | collective-permute-start | bytes 6291464 | tf_op jit(solution)/shard_map/ppermute | solution.py:10
  35.6 38.8 %collective-permute-done.2 = f32[256,2048]{1,0:T(8,128)} collective-permute-done((f32[256,2048]{1,0:T(8,128)S(1)}, f32[256,2048]{1,0:T(8,128)}, u32[]{:S(2)}, u32[]{:S(2)}) %collective-permute-start.2) | collective-permute-done | bytes 2097184 | tf_op jit(solution)/shard_map/ppermute | solution.py:10
  74.4 3.2 %add.33 = f32[256,2048]{1,0:T(8,128)} add(f32[256,2048]{1,0:T(8,128)S(1)} %convolution_subtract_fusion, f32[256,2048]{1,0:T(8,128)} %collective-permute-done.2) | non-fusion elementwise | flops 524288 | bytes 6291456 | tf_op jit(solution)/shard_map/add | solution.py:44
  77.6 1.6 collective-permute-start.3
  79.2 41.3 %collective-permute-done = f32[256,2048]{1,0:T(8,128)} collective-permute-done((f32[256,2048]{1,0:T(8,128)}, f32[256,2048]{1,0:T(8,128)}, u32[]{:S(2)}, u32[]{:S(2)}) %collective-permute-start) | collective-permute-done | bytes 2097184 | tf_op jit(solution)/shard_map/ppermute | solution.py:10
  120.5 2.5 %dynamic-slice_add_fusion = f32[256,2048]{1,0:T(8,128)S(1)} fusion(f32[256,2048]{1,0:T(8,128)} %collective-permute-done, f32[256,4096]{1,0:T(8,128)} %fusion.3, s32[]{:T(128)S(6)} %select_n.12), kind=kLoop, calls=%fused_computation.4 | loop fusion | flops 524288 | bytes 6291460 | tf_op jit(solution)/shard_map/add | solution.py:21
  122.9 1.0 constant_dynamic-slice_fusion
  124.0 0.0 collective-permute-start.1
  124.0 62.8 %collective-permute-done.1 = f32[256,1024]{1,0:T(8,128)} collective-permute-done((f32[256,1024]{1,0:T(8,128)}, f32[256,1024]{1,0:T(8,128)}, u32[]{:S(2)}, u32[]{:S(2)}) %collective-permute-start.1) | collective-permute-done | bytes 1048608 | tf_op jit(solution)/shard_map/ppermute | solution.py:10
  186.7 0.0 collective-permute-done.3
  186.7 0.0 all-gather.4.cloned.1.call-done
  186.7 8.1 %add_bitcast_fusion = f32[1,256,1024]{2,1,0:T(8,128)} fusion(f32[256,1024]{1,0:T(8,128)} %collective-permute-done.1, f32[256,2048]{1,0:T(8,128)S(1)} %dynamic-slice_add_fusion, s32[]{:T(128)S(6)} %select_n.14, bf16[1,2048,1024]{2,1,0:T(8,128)(2,1)} %all-gather.4.cloned.1.call-done, f32[256,2048]{1,0:T(8,128)} %add.33, f32[256,2048]{1,0:T(8,128)} %collective-permute-done.3), kind=kOutput, calls=%fused_computation.7 | convolution fusion | flops 6443499520 | bytes 11534340 | tf_op jit(solution)/shard_map/dot_general | solution.py:47
Async XLA Ops:
  6.5 20.7 %copy-start = (bf16[1,128,4096]{2,1,0:T(8,128)(2,1)S(1)}, bf16[1,128,4096]{2,1,0:T(8,128)(2,1)}, u32[]{:S(2)}) copy-start(bf16[1,128,4096]{2,1,0:T(8,128)(2,1)} %param.11) | copy-start | bytes 3145732
  6.5 180.2 %all-gather.4.cloned.1.call-start = ((), (), s32[]{:S(2)}) async-start(), calls=%async_computation | async-start | bytes 4718592 | tf_op jit(solution)/shard_map/all_gather | solution.py:49
  25.0 2.3 %copy-start.1 = (bf16[1,256,128]{2,1,0:T(8,128)(2,1)S(1)}, bf16[1,256,128]{2,1,0:T(8,128)(2,1)}, u32[]{:S(2)}) copy-start(bf16[1,256,128]{2,1,0:T(8,128)(2,1)} %param.7) | copy-start | bytes 196612
  27.2 47.2 %collective-permute-start.2 = (f32[256,2048]{1,0:T(8,128)S(1)}, f32[256,2048]{1,0:T(8,128)}, u32[]{:S(2)}, u32[]{:S(2)}) collective-permute-start(f32[256,2048]{1,0:T(8,128)S(1)} %convolution_subtract_fusion), channel_id=1, source_target_pairs={{0,8},{8,0},{16,24},{24,16},{32,40},{40,32},{48,56},{56,48},{64,72... | collective-permute-start | bytes 6291464 | tf_op jit(solution)/shard_map/ppermute | solution.py:10
  33.1 87.4 %collective-permute-start = (f32[256,2048]{1,0:T(8,128)}, f32[256,2048]{1,0:T(8,128)}, u32[]{:S(2)}, u32[]{:S(2)}) collective-permute-start(f32[256,2048]{1,0:T(8,128)} %constant_dynamic-slice_fusion.1), channel_id=1, source_target_pairs={{0,16},{8,24},{16,0},{24,8},{32,48},{40,56},{48,32},{56,40},{64,80... | collective-permute-start | bytes 6291464 | tf_op jit(solution)/shard_map/ppermute | solution.py:10
  77.6 109.1 %collective-permute-start.3 = (f32[256,2048]{1,0:T(8,128)}, f32[256,2048]{1,0:T(8,128)}, u32[]{:S(2)}, u32[]{:S(2)}) collective-permute-start(f32[256,2048]{1,0:T(8,128)} %add.33), channel_id=1, source_target_pairs={{0,16},{8,24},{16,0},{24,8},{32,48},{40,56},{48,32},{56,40},{64,80... | collective-permute-start | bytes 6291464 | tf_op jit(solution)/shard_map/ppermute | solution.py:10
  124.0 62.8 %collective-permute-start.1 = (f32[256,1024]{1,0:T(8,128)}, f32[256,1024]{1,0:T(8,128)}, u32[]{:S(2)}, u32[]{:S(2)}) collective-permute-start(f32[256,1024]{1,0:T(8,128)} %constant_dynamic-slice_fusion), channel_id=1, source_target_pairs={{0,8},{8,0},{16,24},{24,16},{32,40},{40,32},{48,56},{56,48},{64,72... | collective-permute-start | bytes 3145736 | tf_op jit(solution)/shard_map/ppermute | solution.py:10
Sparse Core Ops, SparseCore 0:
  9.2 38.8 all-gather.3
where the time goes:
time: 202 us
  waiting for transfers between devices  144 us (71%)
  blocking collectives  16.4 us (8%)
  between operations  14.1 us (7%)
  matrix products  13 us (6%)
  other arithmetic  6.34 us (3%)
  starting transfers between devices  4.22 us (2%)
  local copies, waits for them, and re-layouts  4.18 us (2%)
    ppermute x4, waiting for transfers between devices, partner(): lax.ppermute(value, axis, [(i, i ^ 1 << bit) for i in range(lax.axis_size...  143 us
    all_gather x1, blocking collectives, on_device(): lax.all_gather(coup, 'panel', axis=0, tiled=True)  16.4 us
    dot_general x1, matrix products, on_device(): jnp.dot(columns, lax.all_gather(coords, 'panel', axis=0, tiled=True).asty...  8.15 us
    ppermute x4, starting transfers between devices, partner(): lax.ppermute(value, axis, [(i, i ^ 1 << bit) for i in range(lax.axis_size...  4.21 us
    dynamic_slice x2, local copies, waits for them, and re-layouts, modal_reduce(): other = lax.dynamic_slice_in_dim(current, (1 - my_bit) * half, half, 1)  4.17 us
  transfers between devices with their start and end apart: 5, of which 3 were waited for; matrix products, arithmetic and copies ran while one was open for 8% of the time, Pallas kernels for 0%

commit v1 on v0

v1 whole, which is shorter than its diff:
```python
import jax
import jax.numpy as jnp
from jax import lax
from jax.experimental import pallas as pl
from jax.experimental.pallas import tpu as pltpu
from jax.sharding import PartitionSpec as P

MESH = pl.DeviceIdType.MESH
BF, F32 = jnp.bfloat16, jnp.float32
G = 4
ROWS, NI, M, RL = 256, 2048, 128, 1024
BLK, SUB = 512, 128
QR = 16
COPIES = 80


def kernel(a_hbm, c_hbm, lam_ref, cnt_ref, x_hbm, q_hbm, out_ref,
           abuf, call, sg, qg, xall, rs, rr, mg, mo, ml, ssem, rsem, lsem):
    leaf, panel = lax.axis_index("leaf"), lax.axis_index("panel")
    y, x, core = lax.rem(leaf, G), panel // 2, lax.rem(panel, 2)
    base = leaf - y

    def wrap(v):
        return lax.rem(v + G, G)

    def at_y(d):
        return {"leaf": base + wrap(y + d), "panel": panel}

    def at_x(d):
        return {"leaf": leaf, "panel": wrap(x + d) * 2 + core}

    sibling = {"leaf": leaf, "panel": x * 2 + 1 - core}
    partners = [sibling] + [at_y(d) for d in (1, -1, 2)] + [at_x(d) for d in (1, -1, 2)]

    used = []

    def remote(src, dst, device):
        n = len(used)
        copy = pltpu.make_async_remote_copy(
            src_ref=src, dst_ref=dst, send_sem=ssem.at[n], recv_sem=rsem.at[n],
            device_id=device, device_id_type=MESH)
        copy.start()
        used.append(copy)
        return copy

    def rows_of(d, c=None):
        return pl.multiple_of((wrap(x + d) * 2 + (core if c is None else c)) * ROWS, ROWS)

    def block_rows(d):
        return pl.multiple_of(wrap(x + d) * BLK, BLK)

    order = (0, -1, 1, 2)
    mine = rows_of(0)
    qrow = pl.multiple_of(panel * QR, QR)

    local = [pltpu.make_async_copy(c_hbm.at[0], call.at[pl.ds(mine, ROWS)], lsem.at[0])]
    for j, d in enumerate(order):
        local.append(pltpu.make_async_copy(a_hbm.at[0, :, pl.ds(block_rows(d), BLK)], abuf.at[j], lsem.at[1 + j]))
    local.append(pltpu.make_async_copy(x_hbm.at[0], xall.at[pl.ds(mine, ROWS)], lsem.at[5]))
    local.append(pltpu.make_async_copy(q_hbm.at[0, :, pl.ds(pl.multiple_of(y * RL, RL), RL)], qg.at[0], lsem.at[6]))
    for copy in local:
        copy.start()

    barrier = pltpu.get_barrier_semaphore()
    for device in partners:
        pl.semaphore_signal(barrier, inc=1, device_id=device, device_id_type=MESH)
    pl.semaphore_wait(barrier, len(partners))

    c_sib = remote(c_hbm.at[0], call.at[pl.ds(mine, ROWS)], sibling)
    c_in = {}
    for d in (1, -1, 2):
        c_in[-d if d != 2 else 2] = remote(c_hbm.at[0], call.at[pl.ds(mine, ROWS)], at_x(d))
    q_in = []
    for d in (1, -1, 2):
        slot = (G - d) % G
        q_in.append(remote(
            q_hbm.at[0, pl.ds(qrow, QR), pl.ds(pl.multiple_of(wrap(y + d) * RL, RL), RL)],
            qg.at[slot, pl.ds(qrow, QR)], at_y(d)))
    H = ROWS // 2
    x_in = {}

    def x_half(h):
        return x_hbm.at[0, pl.ds(h * H, H)]

    for d, h in ((1, 0), (-1, 1), (1, 1), (-1, 0)):
        x_in[-d, h] = remote(x_half(h), xall.at[pl.ds(mine + h * H, H)], at_x(d))
    x_sib = remote(x_hbm.at[0], xall.at[pl.ds(mine, ROWS)], sibling)

    local[0].wait()
    keep = (lax.broadcasted_iota(jnp.int32, (1, M), 1) < cnt_ref[0]).astype(F32)
    scale = keep / lam_ref[...]
    sg[0] = (call[pl.ds(mine, ROWS), :].astype(F32) * scale).astype(BF)
    s_in = []
    for d in (1, -1, 2):
        s_in.append(remote(sg.at[0], sg.at[(G - d) % G], at_y(d)))

    r_in = []

    def schur(j):
        local[1 + j].wait()
        got = []
        for d in (1, 3, 2, 0):
            col = pl.multiple_of(wrap(y + d) * SUB, SUB)
            ck = call[pl.ds(pl.multiple_of(block_rows(order[j]) + col, SUB), SUB), :]
            val = abuf[j, :, pl.ds(col, SUB)] - lax.dot_general(
                sg[0], ck, (((1,), (1,)), ((), ())), preferred_element_type=F32)
            if d == 0:
                mo[j] = val
            else:
                rs[j, d - 1] = val.astype(BF)
                got.append(remote(rs.at[j, d - 1], rr.at[j, G - d - 1], at_y(d)))
        r_in.append(got)

    c_sib.wait_recv()
    schur(0)
    c_fwd = {}
    for d in (-1, 1, 2):
        c_in[d].wait_recv()
        r = rows_of(d)
        c_fwd[d] = remote(call.at[pl.ds(r, ROWS)], call.at[pl.ds(r, ROWS)], sibling)
    for j in (1, 2, 3):
        c_fwd[order[j]].wait_recv()
        schur(j)

    for copy in q_in:
        copy.wait_recv()

    def q_piece(d):
        return qg.at[pl.ds(1, 3), pl.ds(pl.multiple_of((wrap(x + d) * 2 + core) * QR, QR), QR)]

    qx_in = {}
    for d in (1, -1, 2):
        qx_in[-d if d != 2 else 2] = remote(q_piece(0), q_piece(0), at_x(d))
    q_sib = [remote(q_piece(0), q_piece(0), sibling)]

    m_in = []

    def reduce(j):
        for copy in r_in[j]:
            copy.wait_recv()
        total = mo[j] + rr[j, 0].astype(F32) + rr[j, 1].astype(F32) + rr[j, 2].astype(F32)
        high = total.astype(BF)
        mg[j, y] = high
        ml[j] = (total - high.astype(F32)).astype(BF)
        m_in.append([remote(mg.at[j, y], mg.at[j, y], at_y(1)), remote(mg.at[j, y], mg.at[j, y], at_y(-1))])

    m_fwd = []

    def forward_m(j):
        fwd = []
        for n, (d, h) in enumerate(((-1, 0), (1, 1))):
            m_in[j][n].wait_recv()
            piece = mg.at[j, wrap(y + d), pl.ds(h * H, H)]
            fwd.append(remote(piece, piece, at_y(-d)))
        m_fwd.append(fwd)

    x_fwd = []
    x_share = {}

    def share(d, h):
        piece = xall.at[pl.ds(rows_of(d) + h * H, H)]
        x_share[d, h] = remote(piece, piece, sibling)

    reduce(0)
    reduce(1)
    for d, h in ((-1, 0), (1, 1)):
        x_in[d, h].wait_recv()
        piece = xall.at[pl.ds(rows_of(d) + h * H, H)]
        x_fwd.append(remote(piece, piece, at_x(-d)))
        share(d, h)
    forward_m(0)
    reduce(2)
    forward_m(1)
    for d in (-1, 1, 2):
        qx_in[d].wait_recv()
        q_sib.append(remote(q_piece(d), q_piece(d), sibling))
    reduce(3)
    for d, h in ((-1, 1), (1, 0)):
        x_in[d, h].wait_recv()
        share(d, h)
    forward_m(2)

    for copy in s_in + q_sib:
        copy.wait_recv()
    local[6].wait()
    scaled = jnp.concatenate([sg[i] for i in range(G)], axis=1)
    out_ref[0] = jnp.dot(scaled, qg[...].reshape(G * M, RL), preferred_element_type=F32)

    def product(j):
        k = block_rows(order[j])
        merged = jnp.concatenate([mg[j, o] for o in range(G)], axis=1)
        out_ref[0] += jnp.dot(merged, xall[pl.ds(k, BLK), :], preferred_element_type=F32)
        own = pl.multiple_of(k + y * SUB, SUB)
        out_ref[0] += jnp.dot(ml[j], xall[pl.ds(own, SUB), :], preferred_element_type=F32)

    def ready(j):
        for copy in m_fwd[j]:
            copy.wait_recv()

    x_sib.wait_recv()
    local[5].wait()
    ready(0)
    product(0)
    forward_m(3)
    for h, copy in enumerate(x_fwd):
        copy.wait_recv()
        share(2, h)
    for j in (1, 2, 3):
        ready(j)
        for h in (0, 1):
            x_share[order[j], h].wait_recv()
        product(j)
    for copy in used:
        copy.wait_send()


def on_device(interface_block, coupling, eigenvalues, mode_counts, interface_coords, modal_coords):
    anywhere = pl.BlockSpec(memory_space=pl.ANY)
    vmem = pl.BlockSpec(memory_space=pltpu.VMEM)
    return pl.pallas_call(
        kernel,
        name="merge_recover",
        out_shape=jax.ShapeDtypeStruct((1, ROWS, RL), F32),
        in_specs=[anywhere, anywhere, vmem, pl.BlockSpec(memory_space=pltpu.SMEM), anywhere, anywhere],
        out_specs=vmem,
        scratch_shapes=[
            pltpu.VMEM((G, ROWS, BLK), F32),
            pltpu.VMEM((NI, M), BF),
            pltpu.VMEM((G, ROWS, M), BF),
            pltpu.VMEM((G, M, RL), BF),
            pltpu.VMEM((NI, RL), BF),
            pltpu.VMEM((G, G - 1, ROWS, SUB), BF),
            pltpu.VMEM((G, G - 1, ROWS, SUB), BF),
            pltpu.VMEM((G, G, ROWS, SUB), BF),
            pltpu.VMEM((G, ROWS, SUB), F32),
            pltpu.VMEM((G, ROWS, SUB), BF),
            pltpu.SemaphoreType.DMA((COPIES,)),
            pltpu.SemaphoreType.DMA((COPIES,)),
            pltpu.SemaphoreType.DMA((7,)),
        ],
        compiler_params=pltpu.CompilerParams(
            collective_id=0, has_side_effects=True, vmem_limit_bytes=40 * 2**20),
        cost_estimate=pl.CostEstimate(flops=1_500_000_000, bytes_accessed=5 * 2**20, transcendentals=0),
    )(interface_block, coupling, eigenvalues, mode_counts, interface_coords, modal_coords)


def solution(mesh):
    placed = (
        P("leaf", "panel", None),
        P("leaf", "panel", None),
        P("leaf", None),
        P("leaf"),
        P("leaf", "panel", None),
        P("leaf", None, None),
    )
    return jax.shard_map(
        on_device, mesh=mesh, in_specs=placed, out_specs=P("leaf", "panel", None), check_vma=False
    )
```

time: 202 us -> 42.9 us (0.21)
  waiting for transfers between devices: 144 us -> 0 us
  Pallas kernels: 0 us -> 35.6 us
  blocking collectives: 16.4 us -> 0 us
  between operations: 14.1 us -> 0.67 us
  matrix products: 13 us -> 0 us
  other arithmetic: 6.34 us -> 0 us
  starting transfers between devices: 4.22 us -> 0 us
  local copies, waits for them, and re-layouts: 4.18 us -> 6.32 us
    ppermute x4 -> x0, waiting for transfers between devices: 143 us -> none  [partner(): lax.ppermute(value, axis, [(i, i ^ 1 << bit) for i in range(lax.axis_size...]
    pallas_call x0 -> x1, Pallas kernels: none -> 35.6 us  [on_device(): pl.pallas_call(kernel, name='merge_recover', out_shape=jax.ShapeDtypeStru...]
    all_gather x1 -> x0, blocking collectives: 16.4 us -> none  [on_device(): lax.all_gather(coup, 'panel', axis=0, tiled=True)]
    dot_general x3 -> x0, matrix products: 13 us -> none  [the longest x1 8.15 us: on_device(): jnp.dot(columns, lax.all_gather(coords, 'panel', axis=0, tiled=True).asty...]
    unnamed x4 -> x11, local copies, waits for them, and re-layouts: 0.01 us -> 6.32 us
    add x2 -> x0, other arithmetic: 5.68 us -> none  [the longest x1 3.21 us: on_device(): merged = merged + partner(merged, 'leaf', level)]
    ppermute x4 -> x0, starting transfers between devices: 4.21 us -> none  [partner(): lax.ppermute(value, axis, [(i, i ^ 1 << bit) for i in range(lax.axis_size...]
    dynamic_slice x2 -> x0, local copies, waits for them, and re-layouts: 4.17 us -> none  [modal_reduce(): other = lax.dynamic_slice_in_dim(current, (1 - my_bit) * half, half, 1)]
  transfers between devices with their start and end apart: 5 -> 0, of which waited for: 3 -> 0; matrix products, arithmetic and copies ran while one was open for 8% -> 0% of each run, Pallas kernels for 0% -> 0%
where the time goes in v1:
time: 42.9 us; the launch traced here: 42.6 us
  Pallas kernels  35.6 us (83%)
  local copies, waits for them, and re-layouts  6.32 us (15%)
  between operations  0.67 us (2%)
    pallas_call x1, Pallas kernels, on_device(): pl.pallas_call(kernel, name='merge_recover', out_shape=jax.ShapeDtypeStru...  35.6 us
    unnamed x11, local copies, waits for them, and re-layouts  6.32 us

profile of v1, /device:TPU:1, one launch (start us, length us, event | category | flops | bytes accessed | tf_op | source)
XLA Modules:
  0.0 42.6 jit_solution(3497052127233556405)
XLA Ops:
  0.7 0.0 copy-start
  0.7 1.6 %copy-done = f32[1,256,2048]{2,1,0:T(8,128)S(1)} copy-done((f32[1,256,2048]{2,1,0:T(8,128)S(1)}, f32[1,256,2048]{2,1,0:T(8,128)}, u32[]{:S(2)}) %copy-start) | copy-done | bytes 2097176
  2.2 0.0 copy-start.1
  2.2 1.2 %copy-done.1 = bf16[1,128,4096]{2,1,0:T(8,128)(2,1)S(1)} copy-done((bf16[1,128,4096]{2,1,0:T(8,128)(2,1)S(1)}, bf16[1,128,4096]{2,1,0:T(8,128)(2,1)}, u32[]{:S(2)}) %copy-start.1) | copy-done | bytes 1048600
  3.5 0.0 copy-start.2
  3.5 1.0 %copy-done.2 = bf16[1,256,1024]{2,1,0:T(8,128)(2,1)S(1)} copy-done((bf16[1,256,1024]{2,1,0:T(8,128)(2,1)S(1)}, bf16[1,256,1024]{2,1,0:T(8,128)(2,1)}, u32[]{:S(2)}) %copy-start.2) | copy-done | bytes 524312
  4.5 0.0 copy-start.3
  4.5 0.8 %copy-done.3 = bf16[1,256,128]{2,1,0:T(8,128)(2,1)S(1)} copy-done((bf16[1,256,128]{2,1,0:T(8,128)(2,1)S(1)}, bf16[1,256,128]{2,1,0:T(8,128)(2,1)}, u32[]{:S(2)}) %copy-start.3) | copy-done | bytes 65560
  5.4 0.0 copy-start.4
  5.4 0.7 %copy-done.4 = f32[1,128]{1,0:T(1,128)S(1)} copy-done((f32[1,128]{1,0:T(1,128)S(1)}, f32[1,128]{1,0:T(1,128)}, u32[]{:S(2)}) %copy-start.4) | copy-done | bytes 536
  6.0 35.6 %merge_recover.1 = f32[1,256,1024]{2,1,0:T(8,128)S(1)} custom-call(f32[1,256,2048]{2,1,0:T(8,128)S(1)} %copy-done, bf16[1,256,128]{2,1,0:T(8,128)(2,1)S(1)} %copy-done.3, f32[1,128]{1,0:T(1,128)S(1)} %copy-done.4, s32[1]{0:T(128)S(6)} %copy.8.cnt_ref, bf16[1,256,1024]{2,1,0:T(8,128)(2,1)S(1)} %copy-done.2, bf16[1,128,4096]{2,1,0:T(8,128)(2,1)S(1)} %copy-done.1), custom_call_target="tpu_custom_call" | custom-call | flops 1500000000 | bytes 5242880 | tf_op jit(solution)/shard_map/merge_recover/pallas_call | solution.py:220
  41.6 1.0 %copy.9 = f32[1,256,1024]{2,1,0:T(8,128)} copy(f32[1,256,1024]{2,1,0:T(8,128)S(1)} %merge_recover.1) | data formatting | bytes 2097152
Async XLA Ops:
  0.7 1.6 %copy-start = (f32[1,256,2048]{2,1,0:T(8,128)S(1)}, f32[1,256,2048]{2,1,0:T(8,128)}, u32[]{:S(2)}) copy-start(f32[1,256,2048]{2,1,0:T(8,128)} %a_hbm.1) | copy-start | bytes 6291460
  2.2 1.2 %copy-start.1 = (bf16[1,128,4096]{2,1,0:T(8,128)(2,1)S(1)}, bf16[1,128,4096]{2,1,0:T(8,128)(2,1)}, u32[]{:S(2)}) copy-start(bf16[1,128,4096]{2,1,0:T(8,128)(2,1)} %q_hbm.1) | copy-start | bytes 3145732
  3.5 1.0 %copy-start.2 = (bf16[1,256,1024]{2,1,0:T(8,128)(2,1)S(1)}, bf16[1,256,1024]{2,1,0:T(8,128)(2,1)}, u32[]{:S(2)}) copy-start(bf16[1,256,1024]{2,1,0:T(8,128)(2,1)} %x_hbm.1) | copy-start | bytes 1572868
  4.5 0.8 %copy-start.3 = (bf16[1,256,128]{2,1,0:T(8,128)(2,1)S(1)}, bf16[1,256,128]{2,1,0:T(8,128)(2,1)}, u32[]{:S(2)}) copy-start(bf16[1,256,128]{2,1,0:T(8,128)(2,1)} %c_hbm.1) | copy-start | bytes 196612
  5.4 0.7 %copy-start.4 = (f32[1,128]{1,0:T(1,128)S(1)}, f32[1,128]{1,0:T(1,128)}, u32[]{:S(2)}) copy-start(f32[1,128]{1,0:T(1,128)} %lam_ref.1) | copy-start | bytes 1540

commit v2 on v0

v2 whole, which is shorter than its diff:
```python
import functools

import jax
import jax.numpy as jnp
from jax import lax
from jax.experimental import pallas as pl
from jax.experimental.pallas import tpu as pltpu
from jax.sharding import PartitionSpec as P

MESH = pl.DeviceIdType.MESH
BF, F32 = jnp.bfloat16, jnp.float32
G = 4
ROWS, NI, M, RL = 256, 2048, 128, 1024
BLK, SUB, QTR = 512, 128, 64
QR = 16
COPIES = 90
OFFSETS = (0, -1, 1, 2)


def kernel(a_hbm, c_hbm, lam_hbm, cnt_hbm, x_hbm, q_hbm, out_ref,
           lam_ref, cnt_ref, abuf, call, sg, qg, xall, rs, rr, near, mg, mo, ml, ssem, rsem, lsem):
    leaf, panel = lax.axis_index("leaf"), lax.axis_index("panel")
    y, x, core = lax.rem(leaf, G), panel // 2, lax.rem(panel, 2)
    base = leaf - y

    def wrap(v):
        return lax.rem(v + G, G)

    def at_y(d):
        return {"leaf": base + wrap(y + d), "panel": panel}

    def at_x(d):
        return {"leaf": leaf, "panel": wrap(x + d) * 2 + core}

    sibling = {"leaf": leaf, "panel": x * 2 + 1 - core}
    partners = [sibling] + [at_y(d) for d in (1, -1, 2)] + [at_x(d) for d in (1, -1)]

    barrier = pltpu.get_barrier_semaphore()
    for device in partners:
        pl.semaphore_signal(barrier, inc=1, device_id=device, device_id_type=MESH)

    used = []

    def remote(src, dst, device):
        n = len(used)
        copy = pltpu.make_async_remote_copy(
            src_ref=src, dst_ref=dst, send_sem=ssem.at[n], recv_sem=rsem.at[n],
            device_id=device, device_id_type=MESH)
        copy.start()
        used.append(copy)
        return copy

    def c_rows(j, first=0, size=ROWS):
        return call.at[pl.ds(pl.multiple_of(j * BLK + core * ROWS + first, SUB), size)]

    def x_rows(j, q=0, n=4):
        return xall.at[pl.ds(pl.multiple_of(j * BLK + core * ROWS + q * QTR, QTR), n * QTR)]

    def q_rows(d, first=0, size=RL):
        row = pl.multiple_of((wrap(x + d) * 2 + core) * QR, QR)
        return qg.at[pl.ds(1, G - 1), pl.ds(row, QR), pl.ds(first, size)]

    local = {}

    def fetch(name, src, dst):
        local[name] = pltpu.make_async_copy(src, dst, lsem.at[len(local)])
        local[name].start()

    fetch("c", c_hbm.at[0], c_rows(0))
    fetch("lam", lam_hbm, lam_ref)
    fetch("cnt", cnt_hbm, cnt_ref)
    for j, d in enumerate(OFFSETS):
        fetch(j, a_hbm.at[0, :, pl.ds(pl.multiple_of(wrap(x + d) * BLK, BLK), BLK)], abuf.at[j])
    fetch("x", x_hbm.at[0], x_rows(0))
    fetch("q", q_hbm.at[0, :, pl.ds(pl.multiple_of(y * RL, RL), RL)], qg.at[0])

    for name in ("c", "lam", "cnt"):
        local[name].wait()
    keep = (lax.broadcasted_iota(jnp.int32, (1, M), 1) < cnt_ref[0]).astype(F32)
    scale = keep / lam_ref[...]
    mine = call[pl.ds(pl.multiple_of(core * ROWS, ROWS), ROWS), :]
    sg[0] = (mine.astype(F32) * scale).astype(BF)

    pl.semaphore_wait(barrier, len(partners))

    got = {}

    def send_coupling():
        got["c0"] = remote(c_hbm.at[0], c_rows(0), sibling)
        got["c-1"] = remote(c_hbm.at[0], c_rows(1), at_x(1))
        got["c1"] = remote(c_hbm.at[0], c_rows(2), at_x(-1))

    def send_coords(way, q):
        src = x_hbm.at[0, pl.ds(q * QTR, QTR)]
        got["x", -way, q] = remote(src, x_rows(1 if way == 1 else 2, q, 1), at_x(way))

    def forward_coords(way, q):
        got["x", -way, q].wait_recv()
        got["x", 2, q] = remote(x_rows(1 if way == 1 else 2, q, 1), x_rows(3, q, 1), at_x(way))

    def share_coords(d, q, n, waits=()):
        for i in waits:
            got["x", d, i].wait_recv()
        j = OFFSETS.index(d)
        got["xs", d, q] = remote(x_rows(j, q, n), x_rows(j, q, n), sibling)

    def share_own_coords():
        got["xs", 0, 0] = remote(x_hbm.at[0], x_rows(0), sibling)

    def send_scaled():
        for way in (1, -1):
            got["s", -way] = remote(sg.at[0], sg.at[(G - way) % G], at_y(way))

    def forward_scaled():
        for way, h in ((1, 0), (-1, 1)):
            got["s", -way].wait_recv()
            piece = pl.ds(h * SUB, SUB)
            got["sf", way] = remote(sg.at[(G - way) % G, piece], sg.at[2, piece], at_y(way))

    def send_modal(d):
        col = pl.multiple_of(wrap(y + d) * RL, RL)
        for far in (0, 2):
            row = pl.ds(pl.multiple_of((wrap(x + far) * 2 + core) * QR, QR), QR)
            got["q", d, far] = remote(q_hbm.at[0, row, pl.ds(col, RL)], qg.at[(G - d) % G, row], at_y(d))

    def share_modal(d):
        got["qs", d] = remote(q_rows(d), q_rows(d), sibling)

    def spread_modal():
        for d in (2, 1, -1):
            got["q", d, 0].wait_recv()
        for way in (1, -1):
            got["qx", -way] = remote(q_rows(0), q_rows(0), at_x(way))
        share_modal(0)
        for d in (2, 1, -1):
            got["q", d, 2].wait_recv()
        share_modal(2)

    def pass_modal():
        for d in (-1, 1):
            got["qx", d].wait_recv()
            share_modal(d)

    def spread_coupling():
        for way, h in ((1, 0), (-1, 1)):
            j = 1 if way == 1 else 2
            got["c-1" if way == 1 else "c1"].wait_recv()
            got["cs", j] = remote(c_rows(j), c_rows(j), sibling)
            got["cf", way] = remote(c_rows(j, h * SUB, SUB), c_rows(3, h * SUB, SUB), at_x(way))

    def share_coupling():
        for way in (1, -1):
            got["cf", way].wait_recv()
        got["cs", 3] = remote(c_rows(3), c_rows(3), sibling)

    def scaled_up(value):
        value = value * 2.0**20
        square = value * value
        return jnp.where(value < 0, -square * square, square * square).astype(BF)

    def scaled_back(code):
        code = code.astype(F32)
        root = jnp.sqrt(jnp.sqrt(jnp.abs(code))) * 2.0**-20
        return jnp.where(code < 0, -root, root)

    top, low = pl.ds(0, SUB), pl.ds(SUB, SUB)

    def schur(j):
        local[j].wait()
        got["c0" if j == 0 else ("cs", j)].wait_recv()
        value = {}
        for d in (2, 1, 3, 0):
            col = pl.multiple_of(wrap(y + d) * SUB, SUB)
            value[d] = abuf[j, :, pl.ds(col, SUB)] - lax.dot_general(
                sg[0], call[pl.ds(pl.multiple_of(j * BLK + col, SUB), SUB), :],
                (((1,), (1,)), ((), ())), preferred_element_type=F32)
        rs[j, 0, 0] = scaled_up(value[2][:SUB])
        rs[j, 0, 1] = scaled_up(value[1][SUB:])
        rs[j, 1, 0] = scaled_up(value[2][SUB:])
        rs[j, 1, 1] = scaled_up(value[3][:SUB])
        near[j, 0] = value[1][:SUB]
        near[j, 1] = value[3][SUB:]
        mo[j] = value[0]
        for n, way in ((0, 1), (1, -1)):
            got["r", j, n] = remote(rs.at[j, n, pl.ds(0, 2)], rr.at[j, n, pl.ds(0, 2)], at_y(way))

    def combine(j):
        for n, way in ((0, 1), (1, -1)):
            got["r", j, n].wait_recv()
            rs[j, n, 2] = scaled_up(near[j, n] + scaled_back(rr[j, n, 0]))
            got["rc", j, n] = remote(rs.at[j, n, 2], rr.at[j, n, 2], at_y(way))

    def reduce(j):
        for n in (0, 1):
            got["rc", j, n].wait_recv()
        for part, a, b in ((top, 2, 1), (low, 1, 2)):
            total = mo[j, part] + scaled_back(rr[j, 0, a]) + scaled_back(rr[j, 1, b])
            high = total.astype(BF)
            mg[j, y, part] = high
            ml[j, part] = (total - high.astype(F32)).astype(BF)
        for way in (1, -1):
            got["m", j, -way] = remote(mg.at[j, y], mg.at[j, y], at_y(way))

    def forward_merged(j):
        for way, h in ((1, 0), (-1, 1)):
            got["m", j, -way].wait_recv()
            piece = mg.at[j, wrap(y - way), pl.ds(h * SUB, SUB)]
            got["mf", j, way] = remote(piece, piece, at_y(way))

    def modal():
        local["q"].wait()
        for name in (("sf", 1), ("sf", -1), ("qs", 0), ("qs", -1), ("qs", 1), ("qs", 2)):
            got[name].wait_recv()
        scaled = jnp.concatenate([sg[i] for i in range(G)], axis=1)
        out_ref[0] = jnp.dot(scaled, qg[...].reshape(G * M, RL), preferred_element_type=F32)

    def product(j):
        for way in (1, -1):
            got["mf", j, way].wait_recv()
        if j == 0:
            local["x"].wait()
        for name in list(got):
            if name[0] == "xs" and name[1] == OFFSETS[j]:
                got[name].wait_recv()
        own = pl.ds(pl.multiple_of(j * BLK + y * SUB, SUB), SUB)
        merged = jnp.concatenate([mg[j, o] for o in range(G)] + [ml[j]], axis=1)
        coords = jnp.concatenate([xall[pl.ds(j * BLK, BLK), :], xall[own, :]], axis=0)
        out_ref[0] += jnp.dot(merged, coords, preferred_element_type=F32)

    send_coupling()
    send_coords(1, 0)
    send_coords(-1, 2)
    send_scaled()
    send_modal(2)
    send_modal(1)
    send_modal(-1)
    schur(0)
    spread_coupling()
    send_coords(1, 1)
    send_coords(-1, 3)
    send_coords(1, 2)
    send_coords(-1, 0)
    send_coords(1, 3)
    send_coords(-1, 1)
    share_own_coords()
    schur(1)
    schur(2)
    forward_scaled()
    combine(0)
    share_coupling()
    spread_modal()
    schur(3)
    combine(1)
    forward_coords(1, 0)
    forward_coords(-1, 2)
    combine(2)
    forward_coords(1, 1)
    forward_coords(-1, 3)
    combine(3)
    reduce(0)
    share_coords(-1, 0, 2)
    share_coords(1, 2, 2)
    reduce(1)
    reduce(2)
    reduce(3)
    share_coords(-1, 2, 2, (2, 3))
    share_coords(1, 0, 2, (0, 1))
    forward_merged(0)
    pass_modal()
    forward_merged(1)
    share_coords(2, 0, 1, (0,))
    share_coords(2, 2, 1, (2,))
    forward_merged(2)
    modal()
    forward_merged(3)
    product(0)
    product(1)
    product(2)
    share_coords(2, 1, 1, (1,))
    share_coords(2, 3, 1, (3,))
    product(3)
    for copy in used:
        copy.wait_send()


def on_device(interface_block, coupling, eigenvalues, mode_counts, interface_coords, modal_coords):
    held = functools.partial(pltpu.with_memory_space_constraint, memory_space=pltpu.HBM)
    hbm = pl.BlockSpec(memory_space=pltpu.HBM)
    return pl.pallas_call(
        kernel,
        name="merge_recover",
        out_shape=jax.ShapeDtypeStruct((1, ROWS, RL), F32),
        in_specs=[hbm] * 6,
        out_specs=pl.BlockSpec(memory_space=pltpu.VMEM),
        scratch_shapes=[
            pltpu.VMEM((1, M), F32),
            pltpu.SMEM((1,), jnp.int32),
            pltpu.VMEM((G, ROWS, BLK), F32),
            pltpu.VMEM((NI, M), BF),
            pltpu.VMEM((G, ROWS, M), BF),
            pltpu.VMEM((G, M, RL), BF),
            pltpu.VMEM((NI, RL), BF),
            pltpu.VMEM((G, 2, 3, SUB, SUB), BF),
            pltpu.VMEM((G, 2, 3, SUB, SUB), BF),
            pltpu.VMEM((G, 2, SUB, SUB), F32),
            pltpu.VMEM((G, G, ROWS, SUB), BF),
            pltpu.VMEM((G, ROWS, SUB), F32),
            pltpu.VMEM((G, ROWS, SUB), BF),
            pltpu.SemaphoreType.DMA((COPIES,)),
            pltpu.SemaphoreType.DMA((COPIES,)),
            pltpu.SemaphoreType.DMA((9,)),
        ],
        compiler_params=pltpu.CompilerParams(
            collective_id=0, has_side_effects=True, vmem_limit_bytes=40 * 2**20),
        cost_estimate=pl.CostEstimate(flops=1_500_000_000, bytes_accessed=5 * 2**20, transcendentals=0),
    )(held(interface_block), held(coupling), held(eigenvalues), mode_counts, held(interface_coords), held(modal_coords))


def solution(mesh):
    placed = (
        P("leaf", "panel", None),
        P("leaf", "panel", None),
        P("leaf", None),
        P("leaf"),
        P("leaf", "panel", None),
        P("leaf", None, None),
    )
    return jax.shard_map(
        on_device, mesh=mesh, in_specs=placed, out_specs=P("leaf", "panel", None), check_vma=False
    )
```

time: 202 us -> 36.5 us (0.18)
  waiting for transfers between devices: 144 us -> 0 us
  Pallas kernels: 0 us -> 34.7 us
  blocking collectives: 16.4 us -> 0 us
  between operations: 14.1 us -> 0.66 us
  matrix products: 13 us -> 0 us
  other arithmetic: 6.34 us -> 0 us
  starting transfers between devices: 4.22 us -> 0 us
  local copies, waits for them, and re-layouts: 4.18 us -> 0.97 us
    ppermute x4 -> x0, waiting for transfers between devices: 143 us -> none  [partner(): lax.ppermute(value, axis, [(i, i ^ 1 << bit) for i in range(lax.axis_size...]
    pallas_call x0 -> x1, Pallas kernels: none -> 34.7 us  [on_device(): pl.pallas_call(kernel, name='merge_recover', out_shape=jax.ShapeDtypeStru...]
    all_gather x1 -> x0, blocking collectives: 16.4 us -> none  [on_device(): lax.all_gather(coup, 'panel', axis=0, tiled=True)]
    dot_general x3 -> x0, matrix products: 13 us -> none  [the longest x1 8.15 us: on_device(): jnp.dot(columns, lax.all_gather(coords, 'panel', axis=0, tiled=True).asty...]
    add x2 -> x0, other arithmetic: 5.68 us -> none  [the longest x1 3.21 us: on_device(): merged = merged + partner(merged, 'leaf', level)]
    ppermute x4 -> x0, starting transfers between devices: 4.21 us -> none  [partner(): lax.ppermute(value, axis, [(i, i ^ 1 << bit) for i in range(lax.axis_size...]
    dynamic_slice x2 -> x0, local copies, waits for them, and re-layouts: 4.17 us -> none  [modal_reduce(): other = lax.dynamic_slice_in_dim(current, (1 - my_bit) * half, half, 1)]
  transfers between devices with their start and end apart: 5 -> 0, of which waited for: 3 -> 0; matrix products, arithmetic and copies ran while one was open for 8% -> 0% of each run, Pallas kernels for 0% -> 0%
where the time goes in v2:
time: 36.5 us; the launch traced here: 36.4 us
  Pallas kernels  34.7 us (95%)
  local copies, waits for them, and re-layouts  0.97 us (3%)
  between operations  0.66 us (2%)
    pallas_call x1, Pallas kernels, on_device(): pl.pallas_call(kernel, name='merge_recover', out_shape=jax.ShapeDtypeStru...  34.7 us
    unnamed x1, local copies, waits for them, and re-layouts  0.97 us

profile of v2, /device:TPU:1, one launch (start us, length us, event | category | flops | bytes accessed | tf_op | source)
XLA Modules:
  0.0 36.4 jit_solution(16669020354702095291)
XLA Ops:
  0.7 34.7 %merge_recover.1 = f32[1,256,1024]{2,1,0:T(8,128)S(1)} custom-call(f32[1,256,2048]{2,1,0:T(8,128)} %a_hbm.1, bf16[1,256,128]{2,1,0:T(8,128)(2,1)} %c_hbm.1, f32[1,128]{1,0:T(1,128)} %lam_hbm.1, s32[1]{0:T(128)S(6)} %copy.8.cnt_hbm, bf16[1,256,1024]{2,1,0:T(8,128)(2,1)} %x_hbm.1, bf16[1,128,4096]{2,1,0:T(8,128)(2,1)} %q_hbm.1), custom_call_target="tpu_custom_call" | custom-call | flops 1500000000 | bytes 5242880 | tf_op jit(solution)/shard_map/merge_recover/pallas_call | solution.py:289
  35.4 1.0 %copy.9 = f32[1,256,1024]{2,1,0:T(8,128)} copy(f32[1,256,1024]{2,1,0:T(8,128)S(1)} %merge_recover.1) | data formatting | bytes 2097152

commit v3 on v2

--- a/solution.py
+++ b/solution.py
@@ -74,13 +74,6 @@
     fetch("x", x_hbm.at[0], x_rows(0))
     fetch("q", q_hbm.at[0, :, pl.ds(pl.multiple_of(y * RL, RL), RL)], qg.at[0])
 
-    for name in ("c", "lam", "cnt"):
-        local[name].wait()
-    keep = (lax.broadcasted_iota(jnp.int32, (1, M), 1) < cnt_ref[0]).astype(F32)
-    scale = keep / lam_ref[...]
-    mine = call[pl.ds(pl.multiple_of(core * ROWS, ROWS), ROWS), :]
-    sg[0] = (mine.astype(F32) * scale).astype(BF)
-
     pl.semaphore_wait(barrier, len(partners))
 
     got = {}
@@ -108,14 +101,19 @@
         got["xs", 0, 0] = remote(x_hbm.at[0], x_rows(0), sibling)
 
     def send_scaled():
+        for name in ("c", "lam", "cnt"):
+            local[name].wait()
+        keep = (lax.broadcasted_iota(jnp.int32, (1, M), 1) < cnt_ref[0]).astype(F32)
+        scale = keep / lam_ref[...]
+        mine = call[pl.ds(pl.multiple_of(core * ROWS, ROWS), ROWS), :]
+        sg[0] = (mine.astype(F32) * scale).astype(BF)
         for way in (1, -1):
             got["s", -way] = remote(sg.at[0], sg.at[(G - way) % G], at_y(way))
 
-    def forward_scaled():
-        for way, h in ((1, 0), (-1, 1)):
-            got["s", -way].wait_recv()
-            piece = pl.ds(h * SUB, SUB)
-            got["sf", way] = remote(sg.at[(G - way) % G, piece], sg.at[2, piece], at_y(way))
+    def forward_scaled(way):
+        got["s", -way].wait_recv()
+        piece = pl.ds(0 if way == 1 else SUB, SUB)
+        got["sf", way] = remote(sg.at[(G - way) % G, piece], sg.at[2, piece], at_y(way))
 
     def send_modal(d):
         col = pl.multiple_of(wrap(y + d) * RL, RL)
@@ -132,21 +130,21 @@
         for way in (1, -1):
             got["qx", -way] = remote(q_rows(0), q_rows(0), at_x(way))
         share_modal(0)
+
+    def share_far_modal():
         for d in (2, 1, -1):
             got["q", d, 2].wait_recv()
         share_modal(2)
 
-    def pass_modal():
-        for d in (-1, 1):
-            got["qx", d].wait_recv()
-            share_modal(d)
-
-    def spread_coupling():
-        for way, h in ((1, 0), (-1, 1)):
-            j = 1 if way == 1 else 2
-            got["c-1" if way == 1 else "c1"].wait_recv()
-            got["cs", j] = remote(c_rows(j), c_rows(j), sibling)
-            got["cf", way] = remote(c_rows(j, h * SUB, SUB), c_rows(3, h * SUB, SUB), at_x(way))
+    def pass_modal(d):
+        got["qx", d].wait_recv()
+        share_modal(d)
+
+    def spread_coupling(way):
+        j, h = (1, 0) if way == 1 else (2, 1)
+        got["c-1" if way == 1 else "c1"].wait_recv()
+        got["cs", j] = remote(c_rows(j), c_rows(j), sibling)
+        got["cf", way] = remote(c_rows(j, h * SUB, SUB), c_rows(3, h * SUB, SUB), at_x(way))
 
     def share_coupling():
         for way in (1, -1):
@@ -201,11 +199,10 @@
         for way in (1, -1):
             got["m", j, -way] = remote(mg.at[j, y], mg.at[j, y], at_y(way))
 
-    def forward_merged(j):
-        for way, h in ((1, 0), (-1, 1)):
-            got["m", j, -way].wait_recv()
-            piece = mg.at[j, wrap(y - way), pl.ds(h * SUB, SUB)]
-            got["mf", j, way] = remote(piece, piece, at_y(way))
+    def forward_merged(j, way):
+        got["m", j, -way].wait_recv()
+        piece = mg.at[j, wrap(y - way), top if way == 1 else low]
+        got["mf", j, way] = remote(piece, piece, at_y(way))
 
     def modal():
         local["q"].wait()
@@ -228,56 +225,64 @@
         out_ref[0] += jnp.dot(merged, coords, preferred_element_type=F32)
 
     send_coupling()
+    send_modal(2)
+    send_coords(-1, 2)
+    send_modal(-1)
     send_coords(1, 0)
-    send_coords(-1, 2)
+    send_modal(1)
     send_scaled()
-    send_modal(2)
-    send_modal(1)
-    send_modal(-1)
     schur(0)
-    spread_coupling()
+    spread_coupling(1)
+    spread_coupling(-1)
+    send_coords(1, 3)
+    spread_modal()
+    schur(1)
     send_coords(1, 1)
     send_coords(-1, 3)
+    schur(2)
+    share_coupling()
+    send_coords(-1, 0)
     send_coords(1, 2)
-    send_coords(-1, 0)
-    send_coords(1, 3)
     send_coords(-1, 1)
-    share_own_coords()
-    schur(1)
-    schur(2)
-    forward_scaled()
     combine(0)
-    share_coupling()
-    spread_modal()
     schur(3)
     combine(1)
+    combine(2)
+    reduce(0)
+    combine(3)
     forward_coords(1, 0)
+    share_own_coords()
     forward_coords(-1, 2)
-    combine(2)
-    forward_coords(1, 1)
-    forward_coords(-1, 3)
-    combine(3)
-    reduce(0)
-    share_coords(-1, 0, 2)
-    share_coords(1, 2, 2)
     reduce(1)
     reduce(2)
     reduce(3)
+    forward_coords(1, 1)
+    forward_scaled(1)
+    forward_coords(-1, 3)
+    forward_merged(0, 1)
+    forward_scaled(-1)
+    share_coords(-1, 0, 2)
+    forward_merged(1, -1)
+    pass_modal(1)
+    forward_merged(2, 1)
+    forward_merged(2, -1)
+    pass_modal(-1)
+    forward_merged(1, 1)
     share_coords(-1, 2, 2, (2, 3))
-    share_coords(1, 0, 2, (0, 1))
-    forward_merged(0)
-    pass_modal()
-    forward_merged(1)
+    share_far_modal()
+    forward_merged(0, -1)
+    share_coords(1, 2, 2)
     share_coords(2, 0, 1, (0,))
     share_coords(2, 2, 1, (2,))
-    forward_merged(2)
+    forward_merged(3, 1)
+    forward_merged(3, -1)
+    share_coords(1, 0, 2, (0, 1))
     modal()
-    forward_merged(3)
-    product(0)
-    product(1)
-    product(2)
     share_coords(2, 1, 1, (1,))
     share_coords(2, 3, 1, (3,))
+    product(2)
+    product(1)
+    product(0)
     product(3)
     for copy in used:
         copy.wait_send()

time: 36.5 us -> 34.4 us (0.942)
  Pallas kernels: 34.7 us -> 32.7 us
    pallas_call x1, Pallas kernels: 34.7 us -> 32.7 us  [on_device(): pl.pallas_call(kernel, name='merge_recover', out_shape=jax.ShapeDtypeStru...]
where the time goes in v3:
time: 34.4 us; the launch traced here: 34.3 us
  Pallas kernels  32.7 us (95%)
  local copies, waits for them, and re-layouts  0.97 us (3%)
  between operations  0.66 us (2%)
    pallas_call x1, Pallas kernels, on_device(): pl.pallas_call(kernel, name='merge_recover', out_shape=jax.ShapeDtypeStru...  32.7 us
    unnamed x1, local copies, waits for them, and re-layouts  0.97 us

profile of v3, /device:TPU:1, one launch (start us, length us, event | category | flops | bytes accessed | tf_op | source)
XLA Modules:
  0.0 34.3 jit_solution(5506143661954484078)
XLA Ops:
  0.7 32.7 %merge_recover.1 = f32[1,256,1024]{2,1,0:T(8,128)S(1)} custom-call(f32[1,256,2048]{2,1,0:T(8,128)} %a_hbm.1, bf16[1,256,128]{2,1,0:T(8,128)(2,1)} %c_hbm.1, f32[1,128]{1,0:T(1,128)} %lam_hbm.1, s32[1]{0:T(128)S(6)} %copy.8.cnt_hbm, bf16[1,256,1024]{2,1,0:T(8,128)(2,1)} %x_hbm.1, bf16[1,128,4096]{2,1,0:T(8,128)(2,1)} %q_hbm.1), custom_call_target="tpu_custom_call" | custom-call | flops 1500000000 | bytes 5242880 | tf_op jit(solution)/shard_map/merge_recover/pallas_call | solution.py:294
  33.4 1.0 %copy.9 = f32[1,256,1024]{2,1,0:T(8,128)} copy(f32[1,256,1024]{2,1,0:T(8,128)S(1)} %merge_recover.1) | data formatting | bytes 2097152

commit v4 on v3

--- a/solution.py
+++ b/solution.py
@@ -17,7 +17,7 @@
 OFFSETS = (0, -1, 1, 2)
 
 
-def kernel(a_hbm, c_hbm, lam_hbm, cnt_hbm, x_hbm, q_hbm, out_ref,
+def kernel(a_hbm, c_hbm, lam_hbm, cnt_hbm, x_hbm, q_hbm, out_ref, last_m, last_x,
            lam_ref, cnt_ref, abuf, call, sg, qg, xall, rs, rr, near, mg, mo, ml, ssem, rsem, lsem):
     leaf, panel = lax.axis_index("leaf"), lax.axis_index("panel")
     y, x, core = lax.rem(leaf, G), panel // 2, lax.rem(panel, 2)
@@ -54,11 +54,8 @@
         return call.at[pl.ds(pl.multiple_of(j * BLK + core * ROWS + first, SUB), size)]
 
     def x_rows(j, q=0, n=4):
-        return xall.at[pl.ds(pl.multiple_of(j * BLK + core * ROWS + q * QTR, QTR), n * QTR)]
-
-    def q_rows(d, first=0, size=RL):
-        row = pl.multiple_of((wrap(x + d) * 2 + core) * QR, QR)
-        return qg.at[pl.ds(1, G - 1), pl.ds(row, QR), pl.ds(first, size)]
+        first = 3 * BLK if j == 3 else j * BLK + core * ROWS
+        return xall.at[pl.ds(pl.multiple_of(first + q * QTR, QTR), n * QTR)]
 
     local = {}
 
@@ -83,19 +80,22 @@
         got["c-1"] = remote(c_hbm.at[0], c_rows(1), at_x(1))
         got["c1"] = remote(c_hbm.at[0], c_rows(2), at_x(-1))
 
-    def send_coords(way, q):
-        src = x_hbm.at[0, pl.ds(q * QTR, QTR)]
-        got["x", -way, q] = remote(src, x_rows(1 if way == 1 else 2, q, 1), at_x(way))
-
-    def forward_coords(way, q):
-        got["x", -way, q].wait_recv()
-        got["x", 2, q] = remote(x_rows(1 if way == 1 else 2, q, 1), x_rows(3, q, 1), at_x(way))
-
-    def share_coords(d, q, n, waits=()):
-        for i in waits:
-            got["x", d, i].wait_recv()
+    def send_coords(way, q, n=1):
+        src = x_hbm.at[0, pl.ds(q * QTR, n * QTR)]
+        got["x", -way, q] = remote(src, x_rows(1 if way == 1 else 2, q, n), at_x(way))
+
+    def forward_coords(way):
+        j, q = (1, 0) if way == 1 else (2, 2)
+        for i in (q, q + 1):
+            got["x", -way, i].wait_recv()
+        got["x", 2, q] = remote(x_rows(j, q, 2), x_rows(3, q, 2), at_x(way))
+
+    def share_coords(d, q, wait=True):
+        if wait:
+            got["x", d, q].wait_recv()
         j = OFFSETS.index(d)
-        got["xs", d, q] = remote(x_rows(j, q, n), x_rows(j, q, n), sibling)
+        there = last_x.at[pl.ds(q * QTR, 2 * QTR)] if j == 3 else x_rows(j, q, 2)
+        got["xs", d, q] = remote(x_rows(j, q, 2), there, sibling)
 
     def share_own_coords():
         got["xs", 0, 0] = remote(x_hbm.at[0], x_rows(0), sibling)
@@ -115,30 +115,31 @@
         piece = pl.ds(0 if way == 1 else SUB, SUB)
         got["sf", way] = remote(sg.at[(G - way) % G, piece], sg.at[2, piece], at_y(way))
 
+    def q_rows(d, n=1):
+        chip = wrap(x + d)
+        first = lax.rem(chip, 2) * (M // 2) + core * (2 * QR) + (chip // 2 * QR if n == 1 else 0)
+        return pl.ds(pl.multiple_of(first, QR), n * QR)
+
     def send_modal(d):
         col = pl.multiple_of(wrap(y + d) * RL, RL)
-        for far in (0, 2):
-            row = pl.ds(pl.multiple_of((wrap(x + far) * 2 + core) * QR, QR), QR)
-            got["q", d, far] = remote(q_hbm.at[0, row, pl.ds(col, RL)], qg.at[(G - d) % G, row], at_y(d))
+        got["q", d] = remote(q_hbm.at[0, q_rows(0, 2), pl.ds(col, RL)], qg.at[(G - d) % G, q_rows(0, 2)], at_y(d))
 
     def share_modal(d):
-        got["qs", d] = remote(q_rows(d), q_rows(d), sibling)
+        piece = qg.at[pl.ds(1, G - 1), q_rows(d, 2)]
+        got["qs", d] = remote(piece, piece, sibling)
 
     def spread_modal():
         for d in (2, 1, -1):
-            got["q", d, 0].wait_recv()
-        for way in (1, -1):
-            got["qx", -way] = remote(q_rows(0), q_rows(0), at_x(way))
+            got["q", d].wait_recv()
+        piece = qg.at[pl.ds(1, G - 1), q_rows(0)]
+        for way in (1, -1):
+            got["qx", -way] = remote(piece, piece, at_x(way))
         share_modal(0)
 
-    def share_far_modal():
-        for d in (2, 1, -1):
-            got["q", d, 2].wait_recv()
-        share_modal(2)
-
-    def pass_modal(d):
-        got["qx", d].wait_recv()
-        share_modal(d)
+    def pass_modal():
+        for d in (-1, 1):
+            got["qx", d].wait_recv()
+        share_modal(1)
 
     def spread_coupling(way):
         j, h = (1, 0) if way == 1 else (2, 1)
@@ -204,12 +205,15 @@
         piece = mg.at[j, wrap(y - way), top if way == 1 else low]
         got["mf", j, way] = remote(piece, piece, at_y(way))
 
+    def add_product(left, right):
+        out_ref[...] += jnp.dot(jnp.concatenate(left, axis=1), right, preferred_element_type=F32)
+
     def modal():
         local["q"].wait()
-        for name in (("sf", 1), ("sf", -1), ("qs", 0), ("qs", -1), ("qs", 1), ("qs", 2)):
+        for name in (("sf", 1), ("sf", -1), ("qs", 0), ("qs", 1)):
             got[name].wait_recv()
-        scaled = jnp.concatenate([sg[i] for i in range(G)], axis=1)
-        out_ref[0] = jnp.dot(scaled, qg[...].reshape(G * M, RL), preferred_element_type=F32)
+        out_ref[...] = jnp.dot(jnp.concatenate([sg[i] for i in range(G)], axis=1),
+                               qg[...].reshape(G * M, RL), preferred_element_type=F32)
 
     def product(j):
         for way in (1, -1):
@@ -220,70 +224,69 @@
             if name[0] == "xs" and name[1] == OFFSETS[j]:
                 got[name].wait_recv()
         own = pl.ds(pl.multiple_of(j * BLK + y * SUB, SUB), SUB)
-        merged = jnp.concatenate([mg[j, o] for o in range(G)] + [ml[j]], axis=1)
-        coords = jnp.concatenate([xall[pl.ds(j * BLK, BLK), :], xall[own, :]], axis=0)
-        out_ref[0] += jnp.dot(merged, coords, preferred_element_type=F32)
+        add_product([mg[j, o] for o in range(G)] + [ml[j]],
+                    jnp.concatenate([xall[pl.ds(j * BLK, BLK), :], xall[own, :]], axis=0))
+
+    def last_product():
+        for way in (1, -1):
+            got["mf", 3, way].wait_recv()
+        last_m[...] = jnp.concatenate([mg[3, 2 - 2 * core], mg[3, 3 - 2 * core]], axis=1)
+        add_product([mg[3, 2 * core], mg[3, 2 * core + 1]], xall[pl.ds(3 * BLK, ROWS), :])
+        for q in (0, 2):
+            got["xs", 2, q].wait_recv()
 
     send_coupling()
+    send_modal(-1)
+    send_modal(1)
     send_modal(2)
+    send_coords(1, 0)
+    send_scaled()
     send_coords(-1, 2)
-    send_modal(-1)
-    send_coords(1, 0)
-    send_modal(1)
-    send_scaled()
+    spread_coupling(-1)
+    spread_coupling(1)
+    share_own_coords()
+    send_coords(1, 1)
     schur(0)
-    spread_coupling(1)
-    spread_coupling(-1)
-    send_coords(1, 3)
-    spread_modal()
+    send_coords(-1, 3)
     schur(1)
-    send_coords(1, 1)
-    send_coords(-1, 3)
     schur(2)
+    send_coords(-1, 0, 2)
+    send_coords(1, 2, 2)
     share_coupling()
-    send_coords(-1, 0)
-    send_coords(1, 2)
-    send_coords(-1, 1)
     combine(0)
     schur(3)
+    spread_modal()
+    forward_coords(1)
     combine(1)
     combine(2)
     reduce(0)
+    forward_coords(-1)
     combine(3)
-    forward_coords(1, 0)
-    share_own_coords()
-    forward_coords(-1, 2)
     reduce(1)
     reduce(2)
     reduce(3)
-    forward_coords(1, 1)
+    forward_scaled(-1)
+    forward_merged(0, -1)
+    forward_merged(0, 1)
+    pass_modal()
     forward_scaled(1)
-    forward_coords(-1, 3)
-    forward_merged(0, 1)
-    forward_scaled(-1)
-    share_coords(-1, 0, 2)
+    share_coords(-1, 0, False)
+    forward_merged(2, -1)
+    share_coords(1, 0)
     forward_merged(1, -1)
-    pass_modal(1)
     forward_merged(2, 1)
-    forward_merged(2, -1)
-    pass_modal(-1)
     forward_merged(1, 1)
-    share_coords(-1, 2, 2, (2, 3))
-    share_far_modal()
-    forward_merged(0, -1)
-    share_coords(1, 2, 2)
-    share_coords(2, 0, 1, (0,))
-    share_coords(2, 2, 1, (2,))
     forward_merged(3, 1)
     forward_merged(3, -1)
-    share_coords(1, 0, 2, (0, 1))
+    share_coords(1, 2, False)
+    share_coords(-1, 2)
+    share_coords(2, 2)
+    share_coords(2, 0)
     modal()
-    share_coords(2, 1, 1, (1,))
-    share_coords(2, 3, 1, (3,))
+    product(0)
     product(2)
     product(1)
-    product(0)
-    product(3)
+    last_product()
     for copy in used:
         copy.wait_send()
 
@@ -291,12 +294,17 @@
 def on_device(interface_block, coupling, eigenvalues, mode_counts, interface_coords, modal_coords):
     held = functools.partial(pltpu.with_memory_space_constraint, memory_space=pltpu.HBM)
     hbm = pl.BlockSpec(memory_space=pltpu.HBM)
-    return pl.pallas_call(
+    vmem = pl.BlockSpec(memory_space=pltpu.VMEM)
+    partial, merged, coords = pl.pallas_call(
         kernel,
         name="merge_recover",
-        out_shape=jax.ShapeDtypeStruct((1, ROWS, RL), F32),
+        out_shape=[
+            jax.ShapeDtypeStruct((ROWS, RL), F32),
+            jax.ShapeDtypeStruct((ROWS, ROWS), BF),
+            jax.ShapeDtypeStruct((ROWS, RL), BF),
+        ],
         in_specs=[hbm] * 6,
-        out_specs=pl.BlockSpec(memory_space=pltpu.VMEM),
+        out_specs=[vmem] * 3,
         scratch_shapes=[
             pltpu.VMEM((1, M), F32),
             pltpu.SMEM((1,), jnp.int32),
@@ -304,7 +312,7 @@
             pltpu.VMEM((NI, M), BF),
             pltpu.VMEM((G, ROWS, M), BF),
             pltpu.VMEM((G, M, RL), BF),
-            pltpu.VMEM((NI, RL), BF),
+            pltpu.VMEM((NI - ROWS, RL), BF),
             pltpu.VMEM((G, 2, 3, SUB, SUB), BF),
             pltpu.VMEM((G, 2, 3, SUB, SUB), BF),
             pltpu.VMEM((G, 2, SUB, SUB), F32),
@@ -319,6 +327,7 @@
             collective_id=0, has_side_effects=True, vmem_limit_bytes=40 * 2**20),
         cost_estimate=pl.CostEstimate(flops=1_500_000_000, bytes_accessed=5 * 2**20, transcendentals=0),
     )(held(interface_block), held(coupling), held(eigenvalues), mode_counts, held(interface_coords), held(modal_coords))
+    return (partial + jnp.dot(merged, coords, preferred_element_type=F32))[None]
 
 
 def solution(mesh):

time: 34.4 us -> 34.1 us (level)
  matrix products: 0 us -> 1.28 us
  local copies, waits for them, and re-layouts: 0.97 us -> 0 us
  Pallas kernels: 32.7 us -> 32.1 us
    dot_general x0 -> x1, matrix products: none -> 1.28 us  [on_device(): return (partial + jnp.dot(merged, coords, preferred_element_type=F32))[None]]
    unnamed x1 -> x0, local copies, waits for them, and re-layouts: 0.97 us -> none
    pallas_call x1, Pallas kernels: 32.7 us -> 32.1 us  [on_device(): pl.pallas_call(kernel, name='merge_recover', out_shape=[jax.ShapeDtypeStr...]
where the time goes in v4:
time: 34.1 us; the launch traced here: 34 us
  Pallas kernels  32.1 us (94%)
  matrix products  1.28 us (4%)
  between operations  0.66 us (2%)
    pallas_call x1, Pallas kernels, on_device(): pl.pallas_call(kernel, name='merge_recover', out_shape=[jax.ShapeDtypeStr...  32.1 us
    dot_general x1, matrix products, on_device(): return (partial + jnp.dot(merged, coords, preferred_element_type=F32))[None]  1.28 us

profile of v4, /device:TPU:1, one launch (start us, length us, event | category | flops | bytes accessed | tf_op | source)
XLA Modules:
  0.0 34.0 jit_solution(10999852645594003443)
XLA Ops:
  0.7 32.1 %merge_recover.1 = (f32[256,1024]{1,0:T(8,128)S(1)}, bf16[256,256]{1,0:T(8,128)(2,1)S(1)}, bf16[256,1024]{1,0:T(8,128)(2,1)S(1)}) custom-call(f32[1,256,2048]{2,1,0:T(8,128)} %a_hbm.1, bf16[1,256,128]{2,1,0:T(8,128)(2,1)} %c_hbm.1, f32[1,128]{1,0:T(1,128)} %lam_hbm.1, s32[1]{0:T(128)S(6)} %copy.7.cnt_hbm, bf16[1,256,1024]{2,1,0:T(8,128)(2,1)} %x_hbm.1, ...), custom_call_target="tpu_custom_call" | custom-call | flops 1500000000 | bytes 5242880 | tf_op jit(solution)/shard_map/merge_recover/pallas_call | solution.py:298
  32.7 1.3 %fusion = f32[1,256,1024]{2,1,0:T(8,128)} fusion(f32[256,1024]{1,0:T(8,128)S(1)} %get-tuple-element.8, bf16[256,256]{1,0:T(8,128)(2,1)S(1)} %get-tuple-element.9, bf16[256,1024]{1,0:T(8,128)(2,1)S(1)} %get-tuple-element.10), kind=kOutput, calls=%fused_computation.1 | convolution fusion | flops 134479872 | bytes 2752512 | tf_op jit(solution)/shard_map/dot_general | solution.py:330
